TPU v7x, 256 devices: a whole 4x4x8 slice. The times are simulated.
256 devices in a mesh: band: 64 (over z, x, core), tm: 4 (over y).
Axes of the slice: x: 4, y: 4, z: 8, core: 2. Of those that a mesh axis runs over, the one named last changes fastest.
Arguments:
- spectra: float32 [64, 64, 16384], P(None, 'band', 'tm'), may hold values from -6 to 6
- newest: float32 [64, 64, 4, 1024], P(None, 'band', 'tm')
- ingest_owner: int32 [64], P('band'), may hold values from 0 to 3
- low_trial: int32 [4, 4096], P(None, 'band'), may hold values from 0 to 7, as said below
- high_trial: int32 [4, 4096], P(None, 'band'), may hold values from 0 to 7, as said below
- delay_table: int32 [4, 4096], P(None, 'band'), may hold values from 0 to 64, as said below
Outputs:
- dedispersed: float32 [256, 16, 16384], P('band', None, 'tm')
Inputs may be any that keep to these rules, and one draw needn't show every extreme that they name: `low_trial`: at level l (row l-1) entry r belongs to trial r % 2^l and names a trial below 2^(l-1); the highest trial of each subband names trial 2^(l-1) - 1. `high_trial`: as low_trial, for the upper half-subband. `delay_table`: at level l the delays are at most 8 * 2^(l-1), reached by the highest trial of each subband.
All inputs are finite; a program needn't handle non-finite values.
Results may differ from a plain program's by a relative error of at most 0.0003.
Values sent between devices are 32-bit elements; how exact they have to be, the bound alone decides.
A program may use at most 64 MiB of HBM per device.

v0:
```python
import jax
import jax.numpy as jnp
from jax import lax
from jax.sharding import PartitionSpec as P

LEVELS = 4
SHIFT = 8


def spread(value, axis, source):
    kept = jnp.where(lax.axis_index(axis) == source, value, 0).astype(value.dtype)
    return lax.psum(kept, axis)


def from_behind(block, axis, distance):
    devices = range(lax.axis_size(axis))
    route = [(i - distance, i) for i in devices if i - distance in devices]
    return lax.ppermute(block, axis, route)


def channel_stats(ingest):
    block_mean = jnp.mean(ingest, axis=-1)
    centred = ingest - block_mean[:, None]
    inv_scale = 1.0 / jnp.sqrt(jnp.mean(centred * centred, axis=-1) + 1e-06)
    return (block_mean, inv_scale)


def delayed_rows(source, shifts, length):
    reach_max = source.shape[1] - length
    shifted = source
    for bit_pos in range(reach_max.bit_length()):
        step_size = 1 << bit_pos
        moved = jnp.concatenate(
            [jnp.zeros((source.shape[0], step_size), source.dtype), shifted[:, :-step_size]], axis=1
        )
        flags = jnp.right_shift(shifts, bit_pos) % 2 == 1
        shifted = jnp.where(flags[:, None], moved, shifted)
    return shifted[:, reach_max:]


def shards(spectra, newest, ingest_owner, low_trial, high_trial, delay_table):
    ingest = newest[:, 0, 0, :]
    root_slot = ingest_owner[0]
    received = spread(ingest, "tm", root_slot)
    block_mean, inv_scale = channel_stats(received)
    normed = (spectra[:, 0, :] - block_mean[:, None]) * inv_scale[:, None]
    chan_dev, time_dev = normed.shape
    moved = lax.all_to_all(
        normed[:, None, :], "band", split_axis=0, concat_axis=1, tiled=True
    ).reshape(chan_dev, time_dev)
    current = moved
    row_ids = jnp.arange(chan_dev, dtype=jnp.int32)
    for layer_idx in range(LEVELS):
        half_span = 2**layer_idx
        span_width = 2 * half_span
        reach_max = SHIFT * half_span
        low_rows = row_ids // span_width * span_width + low_trial[layer_idx]
        odd_rows = current.reshape(chan_dev // span_width, 2, half_span, time_dev)[:, 1].reshape(
            chan_dev // 2, time_dev
        )
        received_rim = from_behind(odd_rows[:, time_dev - reach_max :], "tm", 1)
        extended = jnp.concatenate([received_rim, odd_rows], axis=1)
        odd_index = row_ids // span_width * half_span + high_trial[layer_idx]
        current = current[low_rows] + delayed_rows(
            extended[odd_index], delay_table[layer_idx], time_dev
        )
    return current.reshape(chan_dev // 2**LEVELS, 2**LEVELS, time_dev)


def solution(mesh):
    return jax.shard_map(
        shards,
        mesh=mesh,
        in_specs=(
            P(None, "band", "tm"),
            P(None, "band", "tm", None),
            P("band"),
            P(None, "band"),
            P(None, "band"),
            P(None, "band"),
        ),
        out_specs=P("band", None, "tm"),
        check_vma=False,
    )
```

profile of v0, /device:TPU:64, one launch (start us, length us, event | category | flops | bytes accessed | tf_op | source)
XLA Modules:
  0.0 146.0 jit_solution(2413679411393339932)
XLA Ops:
  7.5 0.8 copy.18
  8.3 50.5 %all-reduce.24.cloned.1.call-done = f32[64,1024]{1,0:T(8,128)} async-done(((f32[64,1024]{1,0:T(8,128)}), f32[64,1024]{1,0:T(8,128)}) %all-reduce.24.cloned.1.call-update) | async-done | bytes 262160 | tf_op jit(solution)/shard_map/psum | solution.py:12
  58.8 1.1 reduce_sum.18
  59.9 1.2 multiply_reduce_fusion
  61.0 2.4 %subtract_multiply_fusion = f32[64,1,4096]{2,1,0:T(1,128)} fusion(f32[64,1,4096]{2,1,0:T(1,128)S(1)} %copy-done, f32[64]{0:T(128)S(1)} %add_rsqrt_fusion, f32[64]{0:T(128)S(1)} %broadcast_multiply_fusion), kind=kLoop, calls=%fused_computation.35 | loop fusion | flops 524288 | bytes 2097664 | tf_op jit(solution)/shard_map/mul | solution.py:46
  63.4 10.5 %all-to-all-start = ((f32[64,1,4096]{2,1,0:T(1,128)}), f32[64,1,4096]{2,1,0:T(1,128)S(1)}, u32[]{:S(2)}, u32[]{:S(2)}) async-start(f32[64,1,4096]{2,1,0:T(1,128)} %subtract_multiply_fusion), calls=%async_computation | async-start | bytes 2097152 | tf_op jit(solution)/shard_map/all_to_all | solution.py:48
  74.1 28.3 %all-to-all-done = f32[64,1,4096]{2,1,0:T(1,128)S(1)} async-done(((f32[64,1,4096]{2,1,0:T(1,128)}), f32[64,1,4096]{2,1,0:T(1,128)S(1)}, u32[]{:S(2)}, u32[]{:S(2)}) %all-to-all-start) | async-done | bytes 1048608 | tf_op jit(solution)/shard_map/all_to_all | solution.py:48
  102.8 2.3 %collective-permute-start = (f32[32,8]{1,0:T(8,128)S(1)}, f32[32,8]{1,0:T(8,128)S(1)}, u32[]{:S(2)}, u32[]{:S(2)}) collective-permute-start(f32[32,8]{1,0:T(8,128)S(1)} %slice.201), channel_id=1, source_target_pairs={{0,1},{1,2},{2,3},{4,5},{5,6},{6,7},{8,9},{9,10},{10,11},{12,13},{... | collective-permute-start | bytes 3080 | tf_op jit(solution)/shard_map/ppermute | solution.py:18
  105.2 0.6 copy.16
  105.8 0.9 gather_fusion
  106.9 1.0 gather_fusion.1
  109.4 0.6 reshape.749
  110.5 4.0 %collective-permute-start.1 = (f32[32,16]{1,0:T(8,128)S(1)}, f32[32,16]{1,0:T(8,128)S(1)}, u32[]{:S(2)}, u32[]{:S(2)}) collective-permute-start(f32[32,16]{1,0:T(8,128)S(1)} %slice.208), channel_id=1, source_target_pairs={{0,1},{1,2},{2,3},{4,5},{5,6},{6,7},{8,9},{9,10},{10,11},{12,13},{... | collective-permute-start | bytes 6152 | tf_op jit(solution)/shard_map/ppermute | solution.py:18
  114.6 0.9 gather_fusion.2
  115.5 0.5 collective-permute-done.1
  116.2 1.0 gather_fusion.3
  119.7 4.4 %collective-permute-start.2 = (f32[32,32]{1,0:T(8,128)S(1)}, f32[32,32]{1,0:T(8,128)S(1)}, u32[]{:S(2)}, u32[]{:S(2)}) collective-permute-start(f32[32,32]{1,0:T(8,128)S(1)} %slice.216), channel_id=1, source_target_pairs={{0,1},{1,2},{2,3},{4,5},{5,6},{6,7},{8,9},{9,10},{10,11},{12,13},{... | collective-permute-start | bytes 12296 | tf_op jit(solution)/shard_map/ppermute | solution.py:18
  124.0 0.9 gather_fusion.4
  125.5 1.0 gather_fusion.5
  128.8 4.2 %collective-permute-start.3 = (f32[32,64]{1,0:T(8,128)S(1)}, f32[32,64]{1,0:T(8,128)S(1)}, u32[]{:S(2)}, u32[]{:S(2)}) collective-permute-start(f32[32,64]{1,0:T(8,128)S(1)} %slice.225), channel_id=1, source_target_pairs={{0,1},{1,2},{2,3},{4,5},{5,6},{6,7},{8,9},{9,10},{10,11},{12,13},{... | collective-permute-start | bytes 24584 | tf_op jit(solution)/shard_map/ppermute | solution.py:18
  133.0 0.9 gather_fusion.6
  133.9 0.5 collective-permute-done.3
  134.6 1.0 gather_fusion.7
  137.8 1.3 fusion
  (67 shorter events, 10.8 us)
Async XLA Ops:
  6.5 54.5 %copy-start = (f32[64,1,4096]{2,1,0:T(1,128)S(1)}, f32[64,1,4096]{2,1,0:T(1,128)}, u32[]{:S(2)}) copy-start(f32[64,1,4096]{2,1,0:T(1,128)} %param.6) | copy-start | bytes 3145732
  6.5 52.2 %all-reduce.24.cloned.1.call-start = ((), (), s32[]{:S(2)}) async-start(), calls=%async_computation.1 | async-start | bytes 524288 | tf_op jit(solution)/shard_map/psum | solution.py:12
  63.4 10.5 %copy-start.2 = (s32[4,64]{1,0:T(4,128)S(1)}, s32[4,64]{1,0:T(4,128)}, u32[]{:S(2)}) copy-start(s32[4,64]{1,0:T(4,128)} %param.9) | copy-start | bytes 3076
  63.4 10.6 %copy-start.3 = (s32[4,64]{1,0:T(4,128)S(1)}, s32[4,64]{1,0:T(4,128)}, u32[]{:S(2)}) copy-start(s32[4,64]{1,0:T(4,128)} %param.10) | copy-start | bytes 3076
  63.4 10.6 %copy-start.1 = (s32[4,64]{1,0:T(4,128)S(1)}, s32[4,64]{1,0:T(4,128)}, u32[]{:S(2)}) copy-start(s32[4,64]{1,0:T(4,128)} %param.11) | copy-start | bytes 3076
  63.4 39.0 %all-to-all-start = ((f32[64,1,4096]{2,1,0:T(1,128)}), f32[64,1,4096]{2,1,0:T(1,128)S(1)}, u32[]{:S(2)}, u32[]{:S(2)}) async-start(f32[64,1,4096]{2,1,0:T(1,128)} %subtract_multiply_fusion), calls=%async_computation | async-start | bytes 2097152 | tf_op jit(solution)/shard_map/all_to_all | solution.py:48
  102.8 3.9 %collective-permute-start = (f32[32,8]{1,0:T(8,128)S(1)}, f32[32,8]{1,0:T(8,128)S(1)}, u32[]{:S(2)}, u32[]{:S(2)}) collective-permute-start(f32[32,8]{1,0:T(8,128)S(1)} %slice.201), channel_id=1, source_target_pairs={{0,1},{1,2},{2,3},{4,5},{5,6},{6,7},{8,9},{9,10},{10,11},{12,13},{... | collective-permute-start | bytes 3080 | tf_op jit(solution)/shard_map/ppermute | solution.py:18
  110.5 5.5 %collective-permute-start.1 = (f32[32,16]{1,0:T(8,128)S(1)}, f32[32,16]{1,0:T(8,128)S(1)}, u32[]{:S(2)}, u32[]{:S(2)}) collective-permute-start(f32[32,16]{1,0:T(8,128)S(1)} %slice.208), channel_id=1, source_target_pairs={{0,1},{1,2},{2,3},{4,5},{5,6},{6,7},{8,9},{9,10},{10,11},{12,13},{... | collective-permute-start | bytes 6152 | tf_op jit(solution)/shard_map/ppermute | solution.py:18
  119.7 5.6 %collective-permute-start.2 = (f32[32,32]{1,0:T(8,128)S(1)}, f32[32,32]{1,0:T(8,128)S(1)}, u32[]{:S(2)}, u32[]{:S(2)}) collective-permute-start(f32[32,32]{1,0:T(8,128)S(1)} %slice.216), channel_id=1, source_target_pairs={{0,1},{1,2},{2,3},{4,5},{5,6},{6,7},{8,9},{9,10},{10,11},{12,13},{... | collective-permute-start | bytes 12296 | tf_op jit(solution)/shard_map/ppermute | solution.py:18
  128.8 5.6 %collective-permute-start.3 = (f32[32,64]{1,0:T(8,128)S(1)}, f32[32,64]{1,0:T(8,128)S(1)}, u32[]{:S(2)}, u32[]{:S(2)}) collective-permute-start(f32[32,64]{1,0:T(8,128)S(1)} %slice.225), channel_id=1, source_target_pairs={{0,1},{1,2},{2,3},{4,5},{5,6},{6,7},{8,9},{9,10},{10,11},{12,13},{... | collective-permute-start | bytes 24584 | tf_op jit(solution)/shard_map/ppermute | solution.py:18
Sparse Core Ops, SparseCore 0:
  9.7 49.0 all-reduce.23
where the time goes:
time: 148 us; the launch traced here: 146 us
  waiting for transfers between devices  80 us (54%)
  starting transfers between devices  25.4 us (17%)
  between operations  14.6 us (10%)
  other arithmetic  14.5 us (10%)
  local copies, waits for them, and re-layouts  11.5 us (8%)
    psum x1, waiting for transfers between devices, spread(): return lax.psum(kept, axis)  50.5 us
    all_to_all x1, waiting for transfers between devices, shards(): lax.all_to_all(normed[:, None, :], 'band', split_axis=0, concat_axis=1, t...  28.3 us
    ppermute x4, starting transfers between devices, from_behind(): return lax.ppermute(block, axis, route)  14.9 us
    all_to_all x1, starting transfers between devices, shards(): lax.all_to_all(normed[:, None, :], 'band', split_axis=0, concat_axis=1, t...  10.5 us
    select_n x18, other arithmetic, delayed_rows(): shifted = jnp.where(flags[:, None], moved, shifted)  6.34 us
    gather x4, local copies, waits for them, and re-layouts, shards(): extended[odd_index]  3.88 us
    gather x4, local copies, waits for them, and re-layouts, shards(): current[low_rows]  3.7 us
  transfers between devices with their start and end apart: 6, of which 5 were waited for; matrix products, arithmetic and copies ran while one was open for 3% of the time, Pallas kernels for 0%

commit v1 on v0

v1 whole, which is shorter than its diff:
```python
import functools

import jax
import jax.numpy as jnp
from jax import lax
from jax.experimental import pallas as pl
from jax.experimental.pallas import tpu as pltpu
from jax.sharding import PartitionSpec as P

LEVELS = 4
NB, NT = 64, 4
NZ, NX, NC = 8, 4, 2
TILES = 32
CHUNK = 8
FIRST = 8
STAT = FIRST + TILES
ROWS = STAT + 8
ORDER = (0, 3, 1, 2)
MESH = pl.DeviceIdType.MESH


def partner(me, step):
    j, r = step % NZ, step // NZ
    dz = (1 - 2 * (j % 2)) * ((j + 1) // 2)
    z, q = me // (NX * NC), me % (NX * NC)
    x, c = q // NC, q % NC
    return ((z + dz + NZ) % NZ) * (NX * NC) + ((x + r // NC) % NX) * NC + (c + r % NC) % NC


def kernel(
    x_ref, newest_ref, owner_ref, low_ref, high_ref, delay_ref, out_ref,
    buf, tail, fresh, gathered, s1, s2, s3, owner, low, high, delay,
    local_sem, table_sem, send_sem, recv_sem, stat_send, stat_recv, halo_send, halo_recv,
):
    me, t = lax.axis_index("band"), lax.axis_index("tm")
    loads = [
        pltpu.make_async_copy(newest_ref, fresh, local_sem.at[0]),
        pltpu.make_async_copy(x_ref.at[:, pl.ds(TILES - CHUNK, CHUNK)], tail.at[:, pl.ds(0, CHUNK)], local_sem.at[1]),
    ]
    tables = [
        pltpu.make_async_copy(src, dst, table_sem.at[i])
        for i, (src, dst) in enumerate(((owner_ref, owner), (low_ref, low), (high_ref, high), (delay_ref, delay)))
    ]
    for copy in loads + tables:
        copy.start()

    barrier = pltpu.get_barrier_semaphore()

    @pl.loop(1, NB)
    def _(i):
        pl.semaphore_signal(barrier, inc=1, device_id={"band": (me + i) % NB}, device_id_type=MESH)

    for i in range(1, NT):
        pl.semaphore_signal(barrier, inc=1, device_id={"tm": (t + i) % NT}, device_id_type=MESH)
    pl.semaphore_wait(barrier, NB - 1 + NT - 1)

    def spans(c):
        if c == TILES // CHUNK - 1:
            return tail, pl.ds(0, CHUNK + 2), pl.ds(FIRST + c * CHUNK, CHUNK + 2)
        return x_ref, pl.ds(c * CHUNK, CHUNK), pl.ds(FIRST + c * CHUNK, CHUNK)

    def send(c):
        src, here, there = spans(c)

        @pl.loop(1, NB)
        def _(i):
            peer = partner(me, i)
            pltpu.make_async_remote_copy(
                src_ref=src.at[peer, here], dst_ref=buf.at[me, there], send_sem=send_sem.at[c],
                recv_sem=recv_sem.at[c], device_id={"band": peer}, device_id_type=MESH,
            ).start()

        pltpu.make_async_copy(src.at[me, here], buf.at[me, there], recv_sem.at[c]).start()

    def arrive(c):
        src, here, there = spans(c)
        pltpu.make_async_copy(src.at[:, here], buf.at[:, there], recv_sem.at[c]).wait()

    send(ORDER[0])

    loads[0].wait()
    block = fresh[...]
    total = jnp.sum(jnp.sum(block, axis=1), axis=-1, keepdims=True)
    mean = total * (1.0 / (8 * 128))
    centred = block - mean[:, :, None]
    power = jnp.sum(jnp.sum(centred * centred, axis=1), axis=-1, keepdims=True) * (1.0 / (8 * 128))
    inv = 1.0 / jnp.sqrt(power + 1e-6)
    gathered[t, 0] = jnp.broadcast_to(mean, (NB, 128))
    gathered[t, 1] = jnp.broadcast_to(inv, (NB, 128))
    stat_copies = []
    for i in range(1, NT):
        stat_copies.append(pltpu.make_async_remote_copy(
            src_ref=gathered.at[t], dst_ref=gathered.at[t], send_sem=stat_send.at[i - 1], recv_sem=stat_recv.at[i - 1],
            device_id={"tm": (t + i) % NT}, device_id_type=MESH,
        ))
        stat_copies[-1].start()
    for copy in tables:
        copy.wait()
    for i in range(1, NT):
        pltpu.make_async_copy(gathered.at[0], gathered.at[0], stat_recv.at[i - 1]).wait()
    chosen = gathered[0]
    for i in range(1, NT):
        chosen = jnp.where(owner[0] == i, gathered[i], chosen)
    loads[1].wait()
    tail[:, CHUNK, :] = chosen[0]
    tail[:, CHUNK + 1, :] = chosen[1]

    for c in ORDER[1:]:
        send(c)

    lane = lax.broadcasted_iota(jnp.int32, (CHUNK, 128), 1)
    sub = lax.broadcasted_iota(jnp.int32, (CHUNK, 128), 0)

    def delayed(high_now, high_before, d):
        return pltpu.roll(jnp.where(lane < 128 - d, high_now, high_before), d, 1)

    def first_level(c):
        now = pl.ds(FIRST + c * CHUNK, CHUNK)
        before = pl.ds(FIRST + c * CHUNK - 1, CHUNK)

        @pl.loop(0, NB // 16)
        def _(g):
            for p in range(8):
                even = g * 16 + 2 * p
                odd = even + 1
                mean_e, inv_e = buf[even, pl.ds(STAT, 1)], buf[even, pl.ds(STAT + 1, 1)]
                mean_o, inv_o = buf[odd, pl.ds(STAT, 1)], buf[odd, pl.ds(STAT + 1, 1)]
                base = (buf[even, now] - mean_e) * inv_e
                n_now = (buf[odd, now] - mean_o) * inv_o
                n_before = (buf[odd, before] - mean_o) * inv_o
                if c == 0:
                    n_before = jnp.where((sub > 0) | (t > 0), n_before, 0.0)
                for k in range(2):
                    s1[even + k, now] = base + delayed(n_now, n_before, delay[0, even + k])

    def later_level(level, src, c, store):
        now = pl.ds(FIRST + c * CHUNK, CHUNK)
        before = pl.ds(FIRST + c * CHUNK - 1, CHUNK)
        half = 2**level

        @pl.loop(0, NB // 16)
        def _(g):
            for p in range(16):
                r = g * 16 + p
                base = g * 16 + p // (2 * half) * (2 * half)
                lo = base + low[level, r]
                hi = base + half + high[level, r]
                store(r, src[lo, now] + delayed(src[hi, now], src[hi, before], delay[level, r]))

    def halo_levels():
        spot = pl.ds(FIRST - 1, 1)

        @pl.loop(0, NB // 16)
        def _(g):
            for p in range(8):
                even = g * 16 + 2 * p
                odd = even + 1
                base = (buf[even, spot] - buf[even, pl.ds(STAT, 1)]) * buf[even, pl.ds(STAT + 1, 1)]
                over = (buf[odd, spot] - buf[odd, pl.ds(STAT, 1)]) * buf[odd, pl.ds(STAT + 1, 1)]
                for k in range(2):
                    s1[even + k, spot] = jnp.where(t > 0, base + pltpu.roll(over, delay[0, even + k], 1), 0.0)

        for level, src, dst in ((1, s1, s2), (2, s2, s3)):
            half = 2**level

            @pl.loop(0, NB // 16)
            def _(g):
                for p in range(16):
                    r = g * 16 + p
                    base = g * 16 + p // (2 * half) * (2 * half)
                    lo = base + low[level, r]
                    hi = base + half + high[level, r]
                    dst[r, spot] = src[lo, spot] + pltpu.roll(src[hi, spot], delay[level, r], 1)

    def levels(c):
        now = pl.ds(FIRST + c * CHUNK, CHUNK)

        def keep(dst):
            def store(r, value):
                dst[r, now] = value
            return store

        def final(r, value):
            out_ref[r, pl.ds(c * CHUNK, CHUNK)] = value

        first_level(c)
        later_level(1, s1, c, keep(s2))
        later_level(2, s2, c, keep(s3))
        later_level(3, s3, c, final)

    arrive(0)
    arrive(3)
    halo = pltpu.make_async_remote_copy(
        src_ref=buf.at[:, pl.ds(STAT - 1, 1)], dst_ref=buf.at[:, pl.ds(FIRST - 1, 1)], send_sem=halo_send,
        recv_sem=halo_recv, device_id={"tm": (t + 1) % NT}, device_id_type=MESH,
    )
    halo.start()
    halo.wait_recv()
    halo_levels()
    levels(0)
    arrive(1)
    levels(1)
    arrive(2)
    levels(2)
    levels(3)

    halo.wait_send()
    for copy in stat_copies:
        copy.wait_send()
    for c in ORDER:
        src, here, there = spans(c)
        pltpu.make_async_copy(src.at[pl.ds(0, NB - 1), here], buf.at[pl.ds(0, NB - 1), there], send_sem.at[c]).wait()


def shards(spectra, newest, ingest_owner, low_trial, high_trial, delay_table):
    state = pltpu.VMEM((NB, ROWS, 128), jnp.float32)
    out = pl.pallas_call(
        kernel,
        out_shape=jax.ShapeDtypeStruct((NB, TILES, 128), jnp.float32),
        in_specs=[pl.BlockSpec(memory_space=pl.ANY)] * 6,
        out_specs=pl.BlockSpec(memory_space=pltpu.VMEM),
        scratch_shapes=[
            state,
            pltpu.VMEM((NB, 2 * CHUNK, 128), jnp.float32),
            pltpu.VMEM((NB, 8, 128), jnp.float32),
            pltpu.VMEM((NT, 2, NB, 128), jnp.float32),
            state, state, state,
            pltpu.SMEM((1,), jnp.int32),
            pltpu.SMEM((LEVELS, NB), jnp.int32),
            pltpu.SMEM((LEVELS, NB), jnp.int32),
            pltpu.SMEM((LEVELS, NB), jnp.int32),
            pltpu.SemaphoreType.DMA((2,)),
            pltpu.SemaphoreType.DMA((4,)),
            pltpu.SemaphoreType.DMA((TILES // CHUNK,)),
            pltpu.SemaphoreType.DMA((TILES // CHUNK,)),
            pltpu.SemaphoreType.DMA((NT - 1,)),
            pltpu.SemaphoreType.DMA((NT - 1,)),
            pltpu.SemaphoreType.DMA,
            pltpu.SemaphoreType.DMA,
        ],
        compiler_params=pltpu.CompilerParams(collective_id=1, has_side_effects=True, vmem_limit_bytes=24 << 20),
    )(spectra.reshape(NB, TILES, 128), newest.reshape(NB, 8, 128), ingest_owner, low_trial, high_trial, delay_table)
    return out.reshape(NB // 16, 16, TILES * 128)


def solution(mesh):
    return jax.shard_map(
        shards,
        mesh=mesh,
        in_specs=(
            P(None, "band", "tm"),
            P(None, "band", "tm", None),
            P("band"),
            P(None, "band"),
            P(None, "band"),
            P(None, "band"),
        ),
        out_specs=P("band", None, "tm"),
        check_vma=False,
    )
```

time: 148 us -> 50.2 us (0.34)
  the two profiles are of different devices: /device:TPU:64 before, /device:TPU:1 now
where the time goes in v1:
time: 50.2 us; the launch traced here: 49.9 us
  Pallas kernels  44.6 us (89%)
  local copies, waits for them, and re-layouts  4.69 us (9%)
  between operations  0.69 us (1%)
    pallas_call x1, Pallas kernels, shards(): pl.pallas_call(kernel, out_shape=jax.ShapeDtypeStruct((NB, TILES, 128), j...  44.6 us
    unnamed x10, local copies, waits for them, and re-layouts  3.53 us
    reshape x1, local copies, waits for them, and re-layouts, shards(): return out.reshape(NB // 16, 16, TILES * 128)  1.16 us

profile of v1, /device:TPU:1, one launch (start us, length us, event | category | flops | bytes accessed | tf_op | source)
XLA Modules:
  0.0 49.9 jit_solution(10413772035222649356)
XLA Ops:
  0.0 0.0 copy-start.3
  0.7 0.0 copy-start.2
  0.7 0.0 copy-done.3
  0.7 0.7 %copy-done.2 = s32[4,64]{1,0:T(4,128)S(1)} copy-done((s32[4,64]{1,0:T(4,128)S(1)}, s32[4,64]{1,0:T(4,128)}, u32[]{:S(2)}) %copy-start.2) | copy-done | bytes 1048
  1.4 0.0 copy-start
  1.4 1.2 %copy-done = f32[64,1,4096]{2,1,0:T(1,128)S(1)} copy-done((f32[64,1,4096]{2,1,0:T(1,128)S(1)}, f32[64,1,4096]{2,1,0:T(1,128)}, u32[]{:S(2)}) %copy-start) | copy-done | bytes 1048600
  2.6 0.0 copy-start.1
  2.6 0.9 %copy-done.1 = f32[64,1,1,1024]{3,2,1,0:T(1,128)S(1)} copy-done((f32[64,1,1,1024]{3,2,1,0:T(1,128)S(1)}, f32[64,1,1,1024]{3,2,1,0:T(1,128)}, u32[]{:S(2)}) %copy-start.1) | copy-done | bytes 262168
  3.5 0.0 copy-start.4
  3.5 0.7 %copy-done.4 = s32[4,64]{1,0:T(4,128)S(1)} copy-done((s32[4,64]{1,0:T(4,128)S(1)}, s32[4,64]{1,0:T(4,128)}, u32[]{:S(2)}) %copy-start.4) | copy-done | bytes 1048
  4.2 44.6 %shard_map.64 = f32[64,32,128]{2,1,0:T(8,128)S(1)} custom-call(f32[64,32,128]{2,1,0:T(8,128)S(1)} %bitcast.2, f32[64,8,128]{2,1,0:T(8,128)S(1)} %bitcast.3, s32[1]{0:T(128)S(6)} %copy.7.owner_ref, s32[4,64]{1,0:T(4,128)S(1)} %copy-done.2, s32[4,64]{1,0:T(4,128)S(1)} %copy-done.3, s32[4,64]{1,0:T(4,128)S(1)} %copy-done.4), custom_call_target="tpu_custom_call" | custom-call | tf_op jit(solution)/shard_map/pallas_call | solution.py:217
  48.8 1.2 %reshape.11 = f32[4,16,4096]{2,1,0:T(8,128)} reshape(f32[64,32,128]{2,1,0:T(8,128)S(1)} %shard_map.64) | data formatting | bytes 2097152 | tf_op jit(solution)/shard_map/reshape | solution.py:243
Async XLA Ops:
  0.0 0.7 %copy-start.3 = (s32[4,64]{1,0:T(4,128)S(1)}, s32[4,64]{1,0:T(4,128)}, u32[]{:S(2)}) copy-start(s32[4,64]{1,0:T(4,128)} %high_ref.1) | copy-start | bytes 3076
  0.7 0.7 %copy-start.2 = (s32[4,64]{1,0:T(4,128)S(1)}, s32[4,64]{1,0:T(4,128)}, u32[]{:S(2)}) copy-start(s32[4,64]{1,0:T(4,128)} %low_ref.1) | copy-start | bytes 3076
  1.4 1.2 %copy-start = (f32[64,1,4096]{2,1,0:T(1,128)S(1)}, f32[64,1,4096]{2,1,0:T(1,128)}, u32[]{:S(2)}) copy-start(f32[64,1,4096]{2,1,0:T(1,128)} %param.6) | copy-start | bytes 3145732
  2.6 0.9 %copy-start.1 = (f32[64,1,1,1024]{3,2,1,0:T(1,128)S(1)}, f32[64,1,1,1024]{3,2,1,0:T(1,128)}, u32[]{:S(2)}) copy-start(f32[64,1,1,1024]{3,2,1,0:T(1,128)} %param.7) | copy-start | bytes 786436
  3.5 0.7 %copy-start.4 = (s32[4,64]{1,0:T(4,128)S(1)}, s32[4,64]{1,0:T(4,128)}, u32[]{:S(2)}) copy-start(s32[4,64]{1,0:T(4,128)} %delay_ref.1) | copy-start | bytes 3076

commit v2 on v1

v2 whole, which is shorter than its diff:
```python
import functools

import jax
import jax.numpy as jnp
from jax import lax
from jax.experimental import pallas as pl
from jax.experimental.pallas import tpu as pltpu
from jax.sharding import PartitionSpec as P

LEVELS = 4
NB, NT = 64, 4
NZ, NQ = 8, 8
TILES = 32
CHUNK = 8
FIRST = 8
STAT = FIRST + TILES
ROWS = STAT + 8
SPANS = ((0, 8), (8, 8), (16, 8), (24, 7))
HEAD = len(SPANS)
PLAN = [(k, c) for c in range(HEAD) for k in range(NZ)]
UNROLL = 4
MESH = pl.DeviceIdType.MESH


def kernel(
    x_ref, newest_ref, owner_ref, low_ref, high_ref, delay_ref, out_ref,
    buf, tail, fresh, gathered, means, invs, s1, s2, s3, owner, low, high, delay,
    local_sem, table_sem, send_sem, recv_sem, stat_send, stat_recv, halo_send, halo_recv,
):
    me, t = lax.axis_index("band"), lax.axis_index("tm")
    loads = [
        pltpu.make_async_copy(newest_ref, fresh, local_sem.at[0]),
        pltpu.make_async_copy(x_ref.at[:, pl.ds(TILES - 1, 1)], tail.at[:, pl.ds(0, 1)], local_sem.at[1]),
    ]
    tables = [
        pltpu.make_async_copy(src, dst, table_sem.at[i])
        for i, (src, dst) in enumerate(((owner_ref, owner), (low_ref, low), (high_ref, high), (delay_ref, delay)))
    ]
    for copy in loads + tables:
        copy.start()

    barrier = pltpu.get_barrier_semaphore()
    for i in range(1, NB):
        peer = me + i
        pl.semaphore_signal(
            barrier, inc=1, device_id={"band": jnp.where(peer < NB, peer, peer - NB)}, device_id_type=MESH
        )
    for i in range(1, NT):
        pl.semaphore_signal(barrier, inc=1, device_id={"tm": (t + i) % NT}, device_id_type=MESH)

    def spans(c):
        if c == HEAD:
            return tail, pl.ds(0, 2), pl.ds(STAT - 1, 2)
        start, size = SPANS[c]
        return x_ref, pl.ds(start, size), pl.ds(FIRST + start, size)

    z = me // NQ
    q = me - z * NQ
    turned = [jnp.where(q + r < NQ, q + r, q + r - NQ) for r in range(NQ)]

    def send(k, c):
        src, here, there = spans(c)

        def one(peer):
            pltpu.make_async_remote_copy(
                src_ref=src.at[peer, here], dst_ref=buf.at[me, there], send_sem=send_sem.at[c],
                recv_sem=recv_sem.at[c], device_id={"band": peer}, device_id_type=MESH,
            ).start()

        pl.when(k != z)(lambda: one(k * NQ + q))
        for r in range(1, NQ):
            one(k * NQ + turned[r])

    def keep_own(c):
        src, here, there = spans(c)
        pltpu.make_async_copy(src.at[me, here], buf.at[me, there], recv_sem.at[c]).start()

    def arrive(c):
        src, here, there = spans(c)
        pltpu.make_async_copy(src.at[:, here], buf.at[:, there], recv_sem.at[c]).wait()

    for c in range(HEAD):
        keep_own(c)

    loads[0].wait()
    block = fresh[...]
    total = jnp.sum(jnp.sum(block, axis=1), axis=-1, keepdims=True)
    mean = total * (1.0 / (8 * 128))
    centred = block - mean[:, :, None]
    power = jnp.sum(jnp.sum(centred * centred, axis=1), axis=-1, keepdims=True) * (1.0 / (8 * 128))
    inv = 1.0 / jnp.sqrt(power + 1e-6)
    row = lax.broadcasted_iota(jnp.int32, (NB, 128), 0)
    column = lax.broadcasted_iota(jnp.int32, (NB, 128), 1)
    both = jnp.where(column == row, mean, 0.0) + jnp.where(column == row + NB, inv, 0.0)
    for copy in tables:
        copy.wait()
    mine = jnp.where(owner[0] == t, jnp.sum(both, axis=0, keepdims=True), 0.0)
    loads[1].wait()
    tail[:, 1, :] = jnp.broadcast_to(mine, (NB, 128))
    pl.semaphore_wait(barrier, NB - 1 + NT - 1)

    for k in range(NZ):
        send(k, HEAD)
    keep_own(HEAD)
    for k, c in PLAN:
        send(k, c)

    lane = lax.broadcasted_iota(jnp.int32, (CHUNK, 128), 1)
    sub = lax.broadcasted_iota(jnp.int32, (CHUNK, 128), 0)

    def delayed(high_now, high_before, d):
        return pltpu.roll(jnp.where(lane < 128 - d, high_now, high_before), d, 1)

    def first_level(c):
        now = pl.ds(FIRST + c * CHUNK, CHUNK)
        before = pl.ds(FIRST + c * CHUNK - 1, CHUNK)

        @pl.loop(0, NB // 16 // UNROLL)
        def _(g):
            for p in range(8 * UNROLL):
                even = g * 16 * UNROLL + 2 * p
                odd = even + 1
                mean_e, inv_e = means[pl.ds(even, 1)], invs[pl.ds(even, 1)]
                mean_o, inv_o = means[pl.ds(odd, 1)], invs[pl.ds(odd, 1)]
                base = (buf[even, now] - mean_e) * inv_e
                n_now = (buf[odd, now] - mean_o) * inv_o
                n_before = (buf[odd, before] - mean_o) * inv_o
                if c == 0:
                    n_before = jnp.where((sub > 0) | (t > 0), n_before, 0.0)
                for k in range(2):
                    s1[even + k, now] = base + delayed(n_now, n_before, delay[0, even + k])

    def later_level(level, src, c, store):
        now = pl.ds(FIRST + c * CHUNK, CHUNK)
        before = pl.ds(FIRST + c * CHUNK - 1, CHUNK)
        half = 2**level

        @pl.loop(0, NB // 16 // UNROLL)
        def _(g):
            for p in range(16 * UNROLL):
                r = g * 16 * UNROLL + p
                base = g * 16 * UNROLL + p // (2 * half) * (2 * half)
                lo = base + low[level, r]
                hi = base + half + high[level, r]
                store(r, src[lo, now] + delayed(src[hi, now], src[hi, before], delay[level, r]))

    def halo_levels():
        spot = pl.ds(FIRST - 1, 1)

        @pl.loop(0, NB // 16 // UNROLL)
        def _(g):
            for p in range(8 * UNROLL):
                even = g * 16 * UNROLL + 2 * p
                odd = even + 1
                base = (buf[even, spot] - means[pl.ds(even, 1)]) * invs[pl.ds(even, 1)]
                over = (buf[odd, spot] - means[pl.ds(odd, 1)]) * invs[pl.ds(odd, 1)]
                for k in range(2):
                    s1[even + k, spot] = jnp.where(t > 0, base + pltpu.roll(over, delay[0, even + k], 1), 0.0)

        for level, src, dst in ((1, s1, s2), (2, s2, s3)):
            half = 2**level

            @pl.loop(0, NB // 16 // UNROLL)
            def _(g):
                for p in range(16 * UNROLL):
                    r = g * 16 * UNROLL + p
                    base = g * 16 * UNROLL + p // (2 * half) * (2 * half)
                    lo = base + low[level, r]
                    hi = base + half + high[level, r]
                    dst[r, spot] = src[lo, spot] + pltpu.roll(src[hi, spot], delay[level, r], 1)

    def levels(c):
        now = pl.ds(FIRST + c * CHUNK, CHUNK)

        def keep(dst):
            def store(r, value):
                dst[r, now] = value
            return store

        def final(r, value):
            out_ref[r, pl.ds(c * CHUNK, CHUNK)] = value

        first_level(c)
        later_level(1, s1, c, keep(s2))
        later_level(2, s2, c, keep(s3))
        later_level(3, s3, c, final)

    arrive(HEAD)
    halo = pltpu.make_async_remote_copy(
        src_ref=buf.at[:, pl.ds(STAT - 1, 1)], dst_ref=buf.at[:, pl.ds(FIRST - 1, 1)], send_sem=halo_send,
        recv_sem=halo_recv, device_id={"tm": (t + 1) % NT}, device_id_type=MESH,
    )
    halo.start()
    stat = buf[:, STAT, :]
    mean = jnp.sum(jnp.where(column == me, stat, 0.0), axis=1, keepdims=True)
    inv = jnp.sum(jnp.where(column == me + NB, stat, 0.0), axis=1, keepdims=True)
    both = jnp.where(column == row, mean, 0.0) + jnp.where(column == row + NB, inv, 0.0)
    gathered[pl.ds(t, 1)] = jnp.sum(both, axis=0, keepdims=True)[None]
    stat_copies = []
    for i in range(1, NT):
        stat_copies.append(pltpu.make_async_remote_copy(
            src_ref=gathered.at[t], dst_ref=gathered.at[t], send_sem=stat_send.at[i - 1], recv_sem=stat_recv.at[i - 1],
            device_id={"tm": (t + i) % NT}, device_id_type=MESH,
        ))
        stat_copies[-1].start()
    for copy in stat_copies:
        copy.wait_recv()
    stat = gathered[0]
    for i in range(1, NT):
        stat = stat + gathered[i]
    mean = jnp.sum(jnp.where(column == row, stat, 0.0), axis=1, keepdims=True)
    inv = jnp.sum(jnp.where(column == row + NB, stat, 0.0), axis=1, keepdims=True)
    means[...] = jnp.broadcast_to(mean, (NB, 128))
    invs[...] = jnp.broadcast_to(inv, (NB, 128))
    halo.wait_recv()
    halo_levels()
    for c, (start, size) in enumerate(SPANS):
        arrive(c)
        for block in range(start // CHUNK, (start + size + 1) // CHUNK):
            levels(block)

    halo.wait_send()
    for copy in stat_copies:
        copy.wait_send()
    for c in range(HEAD + 1):
        src, here, there = spans(c)
        pltpu.make_async_copy(src.at[pl.ds(0, NB - 1), here], buf.at[pl.ds(0, NB - 1), there], send_sem.at[c]).wait()


def shards(spectra, newest, ingest_owner, low_trial, high_trial, delay_table):
    operands = [spectra.reshape(NB, TILES, 128), newest.reshape(NB, 8, 128), ingest_owner, low_trial, high_trial, delay_table]
    operands = [a if a.size == 1 else pltpu.with_memory_space_constraint(a, pltpu.HBM) for a in operands]
    state = pltpu.VMEM((NB, ROWS, 128), jnp.float32)
    out = pl.pallas_call(
        kernel,
        out_shape=jax.ShapeDtypeStruct((NB, TILES, 128), jnp.float32),
        in_specs=[pl.BlockSpec(memory_space=pl.ANY)] * 6,
        out_specs=pl.BlockSpec(memory_space=pltpu.VMEM),
        scratch_shapes=[
            state,
            pltpu.VMEM((NB, 8, 128), jnp.float32),
            pltpu.VMEM((NB, 8, 128), jnp.float32),
            pltpu.VMEM((NT, 1, 128), jnp.float32),
            pltpu.VMEM((NB, 128), jnp.float32),
            pltpu.VMEM((NB, 128), jnp.float32),
            state, state, state,
            pltpu.SMEM((1,), jnp.int32),
            pltpu.SMEM((LEVELS, NB), jnp.int32),
            pltpu.SMEM((LEVELS, NB), jnp.int32),
            pltpu.SMEM((LEVELS, NB), jnp.int32),
            pltpu.SemaphoreType.DMA((2,)),
            pltpu.SemaphoreType.DMA((4,)),
            pltpu.SemaphoreType.DMA((HEAD + 1,)),
            pltpu.SemaphoreType.DMA((HEAD + 1,)),
            pltpu.SemaphoreType.DMA((NT - 1,)),
            pltpu.SemaphoreType.DMA((NT - 1,)),
            pltpu.SemaphoreType.DMA,
            pltpu.SemaphoreType.DMA,
        ],
        compiler_params=pltpu.CompilerParams(collective_id=1, has_side_effects=True, vmem_limit_bytes=24 << 20),
    )(*operands)
    return out.reshape(NB // 16, 16, TILES * 128)


def solution(mesh):
    return jax.shard_map(
        shards,
        mesh=mesh,
        in_specs=(
            P(None, "band", "tm"),
            P(None, "band", "tm", None),
            P("band"),
            P(None, "band"),
            P(None, "band"),
            P(None, "band"),
        ),
        out_specs=P("band", None, "tm"),
        check_vma=False,
    )
```

time: 50.2 us -> 38.3 us (0.76)
  the two profiles are of different devices: /device:TPU:1 before, /device:TPU:64 now
where the time goes in v2:
time: 38.3 us; the launch traced here: 37.9 us
  Pallas kernels  36.1 us (94%)
  local copies, waits for them, and re-layouts  1.16 us (3%)
  between operations  0.66 us (2%)
    pallas_call x1, Pallas kernels, shards(): pl.pallas_call(kernel, out_shape=jax.ShapeDtypeStruct((NB, TILES, 128), j...  36.1 us
    reshape x1, local copies, waits for them, and re-layouts, shards(): return out.reshape(NB // 16, 16, TILES * 128)  1.16 us

profile of v2, /device:TPU:64, one launch (start us, length us, event | category | flops | bytes accessed | tf_op | source)
XLA Modules:
  0.0 37.9 jit_solution(10529510458110373491)
XLA Ops:
  0.7 36.1 %shard_map.64 = f32[64,32,128]{2,1,0:T(8,128)S(1)} custom-call(f32[64,32,128]{2,1,0:T(8,128)} %bitcast.2, f32[64,8,128]{2,1,0:T(8,128)} %bitcast.3, s32[1]{0:T(128)S(6)} %copy.7.owner_ref, s32[4,64]{1,0:T(4,128)} %low_ref.1, s32[4,64]{1,0:T(4,128)} %high_ref.1, s32[4,64]{1,0:T(4,128)} %delay_ref.1), custom_call_target="tpu_custom_call" | custom-call | tf_op jit(solution)/shard_map/pallas_call | solution.py:234
  36.7 1.2 %reshape.11 = f32[4,16,4096]{2,1,0:T(8,128)} reshape(f32[64,32,128]{2,1,0:T(8,128)S(1)} %shard_map.64) | data formatting | bytes 2097152 | tf_op jit(solution)/shard_map/reshape | solution.py:262

commit v3 on v0

v3 whole, which is shorter than its diff:
```python
import functools

import jax
import jax.numpy as jnp
from jax import lax
from jax.experimental import pallas as pl
from jax.experimental.pallas import tpu as pltpu
from jax.sharding import PartitionSpec as P

LEVELS = 4
NB, NT = 64, 4
NZ, NQ = 8, 8
TILES = 32
CHUNK = 8
FIRST = 8
ROWS = FIRST + TILES
SPANS = ((0, 16), (16, 15))
HEAD = len(SPANS)
PLAN = [(k, c) for c in range(HEAD) for k in range(NZ)]
MESH = pl.DeviceIdType.MESH


def kernel(
    x_ref, newest_ref, owner_ref, low_ref, high_ref, delay_ref, out_ref,
    buf, own, packed, head, tiles, before_first, stat_q, fresh, stat_t, means, invs, s1, s2, s3, low, high, delay,
    local_sem, send_sem, recv_sem, z_send, z_recv, q_send, q_recv, t_send, t_recv, halo_send, halo_recv,
):
    me, t = lax.axis_index("band"), lax.axis_index("tm")
    z = me // NQ
    q = me - z * NQ
    barrier = pltpu.get_barrier_semaphore()
    turned = [jnp.where(q + r < NQ, q + r, q + r - NQ) for r in range(NQ)]
    t_peers = [jnp.where(t + i < NT, t + i, t + i - NT) for i in range(1, NT)]
    for i in range(1, NB):
        peer = jnp.where(me + i < NB, me + i, me + i - NB)
        pl.semaphore_signal(barrier, inc=1, device_id={"band": peer}, device_id_type=MESH)
    for k in t_peers:
        pl.semaphore_signal(barrier, inc=1, device_id={"tm": k}, device_id_type=MESH)

    load = pltpu.make_async_copy(newest_ref, fresh, local_sem.at[0])
    load.start()
    last = pltpu.make_async_copy(x_ref.at[:, pl.ds(TILES - 1, 1)], own.at[:, pl.ds(0, 1)], local_sem.at[4])
    last.start()
    tables = [
        pltpu.make_async_copy(src, dst, local_sem.at[1 + i])
        for i, (src, dst) in enumerate(((low_ref, low), (high_ref, high), (delay_ref, delay)))
    ]
    for copy in tables:
        copy.start()

    def spot(c):
        start, size = SPANS[c]
        return x_ref, pl.ds(start, size), pl.ds(FIRST + start, size)

    def send(k, c):
        src, here, there = spot(c)

        def one(peer):
            pltpu.make_async_remote_copy(
                src_ref=src.at[peer, here], dst_ref=buf.at[me, there], send_sem=send_sem.at[c],
                recv_sem=recv_sem.at[c], device_id={"band": peer}, device_id_type=MESH,
            ).start()

        pl.when(k != z)(lambda: one(k * NQ + q))
        for r in range(1, NQ):
            one(k * NQ + turned[r])

    def keep_own(c):
        src, here, there = spot(c)
        pltpu.make_async_copy(src.at[me, here], buf.at[me, there], recv_sem.at[c]).start()

    def arrive(c):
        src, here, there = spot(c)
        pltpu.make_async_copy(src.at[:, here], buf.at[:, there], recv_sem.at[c]).wait()

    for c in range(HEAD):
        keep_own(c)

    row = lax.broadcasted_iota(jnp.int32, (NB, 128), 0)
    column = lax.broadcasted_iota(jnp.int32, (NB, 128), 1)

    def as_row(mean, inv):
        both = jnp.where(column == row, mean, 0.0) + jnp.where(column == row + NB, inv, 0.0)
        return jnp.sum(both, axis=0, keepdims=True)

    def as_columns(stat, first):
        mean = jnp.sum(jnp.where(column == first, stat, 0.0), axis=1, keepdims=True)
        inv = jnp.sum(jnp.where(column == first + NB, stat, 0.0), axis=1, keepdims=True)
        return mean, inv

    load.wait()
    block = fresh[...]
    mean = jnp.sum(jnp.sum(block, axis=1), axis=-1, keepdims=True) * (1.0 / (8 * 128))
    centred = block - mean[:, :, None]
    power = jnp.sum(jnp.sum(centred * centred, axis=1), axis=-1, keepdims=True) * (1.0 / (8 * 128))
    inv = 1.0 / jnp.sqrt(power + 1e-6)
    mine = jnp.where(owner_ref[0] == t, as_row(mean, inv), 0.0)
    last.wait()
    for k in range(NZ):
        packed[k, pl.ds(0, NQ)] = own[pl.ds(k * NQ, NQ), 0, :]
        packed[k, pl.ds(NQ, 1)] = mine
    pl.semaphore_wait(barrier, NB - 1 + NT - 1)

    head_copies = []
    for i in range(1, NZ):
        k = jnp.where(z + i < NZ, z + i, z + i - NZ)
        head_copies.append(pltpu.make_async_remote_copy(
            src_ref=packed.at[k, pl.ds(0, NQ + 1)], dst_ref=head.at[z, pl.ds(0, NQ + 1)], send_sem=z_send,
            recv_sem=z_recv, device_id={"band": k * NQ + q}, device_id_type=MESH,
        ))
        head_copies[-1].start()
    for k, c in PLAN:
        send(k, c)
    head[z, pl.ds(0, NQ + 1)] = packed[z, pl.ds(0, NQ + 1)]

    lane = lax.broadcasted_iota(jnp.int32, (CHUNK, 128), 1)
    sub = lax.broadcasted_iota(jnp.int32, (CHUNK, 128), 0)

    def delayed(high_now, high_before, d):
        return pltpu.roll(jnp.where(lane < 128 - d, high_now, high_before), d, 1)

    def normed(r, where):
        return (buf[r, where] - means[pl.ds(r, 1)]) * invs[pl.ds(r, 1)]

    def pick(level, r):
        half = 2**level
        base = r // (2 * half) * (2 * half)
        return base + low[level, r], base + half + high[level, r]

    def levels(blocks):
        nows = [pl.ds(FIRST + block * CHUNK, CHUNK) for block in blocks]
        befores = [pl.ds(FIRST + block * CHUNK - 1, CHUNK) for block in blocks]
        for even in range(0, NB, 2):
            for block, now, before in zip(blocks, nows, befores):
                base, n_now, n_before = normed(even, now), normed(even + 1, now), normed(even + 1, before)
                if block == 0:
                    n_before = jnp.where((sub > 0) | (t > 0), n_before, 0.0)
                for k in range(2):
                    s1[even + k, now] = base + delayed(n_now, n_before, delay[0, even + k])
        for level, src, dst in ((1, s1, s2), (2, s2, s3), (3, s3, None)):
            for r in range(NB):
                lo, hi = pick(level, r)
                for block, now, before in zip(blocks, nows, befores):
                    value = src[lo, now] + delayed(src[hi, now], src[hi, before], delay[level, r])
                    if dst is None:
                        out_ref[r, pl.ds(block * CHUNK, CHUNK)] = value
                    else:
                        dst[r, now] = value

    def halo_levels():
        tile = pl.ds(FIRST - 1, 1)
        for even in range(0, NB, 2):
            base, over = normed(even, tile), normed(even + 1, tile)
            for k in range(2):
                s1[even + k, tile] = jnp.where(t > 0, base + pltpu.roll(over, delay[0, even + k], 1), 0.0)
        for level, src, dst in ((1, s1, s2), (2, s2, s3)):
            for r in range(NB):
                lo, hi = pick(level, r)
                dst[r, tile] = src[lo, tile] + pltpu.roll(src[hi, tile], delay[level, r], 1)

    landed = head.at[pl.ds(0, NZ - 1), pl.ds(0, NQ + 1)]
    pltpu.make_async_copy(landed, landed, z_recv).wait()
    for r in range(1, NQ):
        there = {"band": z * NQ + turned[r]}
        for i, (src, dst) in enumerate((
            (head.at[:, pl.ds(turned[r], 1)], tiles.at[:, pl.ds(q, 1)]), (head.at[:, pl.ds(NQ, 1)], stat_q.at[:, pl.ds(q, 1)])
        )):
            pltpu.make_async_remote_copy(
                src_ref=src, dst_ref=dst, send_sem=q_send.at[i], recv_sem=q_recv.at[i], device_id=there, device_id_type=MESH
            ).start()
    tiles[:, pl.ds(q, 1)] = head[:, pl.ds(q, 1)]
    stat_q[:, pl.ds(q, 1)] = head[:, pl.ds(NQ, 1)]
    for i, dst in enumerate((tiles, stat_q)):
        part = dst.at[:, pl.ds(0, NQ - 1)]
        pltpu.make_async_copy(part, part, q_recv.at[i]).wait()

    halo = pltpu.make_async_remote_copy(
        src_ref=tiles, dst_ref=before_first, send_sem=halo_send, recv_sem=halo_recv, device_id={"tm": t_peers[0]},
        device_id_type=MESH,
    )
    halo.start()
    stat_t[pl.ds(t, 1)] = as_row(*as_columns(stat_q[...].reshape(NB, 128), me))[None]
    t_copies = []
    for i, k in enumerate(t_peers):
        t_copies.append(pltpu.make_async_remote_copy(
            src_ref=stat_t.at[t], dst_ref=stat_t.at[t], send_sem=t_send.at[i], recv_sem=t_recv.at[i],
            device_id={"tm": k}, device_id_type=MESH,
        ))
        t_copies[-1].start()
    for copy in t_copies:
        copy.wait_recv()
    stat = stat_t[0]
    for i in range(1, NT):
        stat = stat + stat_t[i]
    mean, inv = as_columns(stat, row)
    means[...] = jnp.broadcast_to(mean, (NB, 128))
    invs[...] = jnp.broadcast_to(inv, (NB, 128))
    for copy in tables:
        copy.wait()
    halo.wait_recv()
    buf[:, FIRST - 1, :] = before_first[...].reshape(NB, 128)
    buf[:, ROWS - 1, :] = tiles[...].reshape(NB, 128)
    halo_levels()
    for c, (start, size) in enumerate(SPANS):
        arrive(c)
        levels(range(start // CHUNK, (start + size + 1) // CHUNK))

    halo.wait_send()
    for copy in t_copies:
        copy.wait_send()
    pltpu.make_async_copy(landed, landed, z_send).wait()
    for i, dst in enumerate((tiles, stat_q)):
        part = dst.at[:, pl.ds(0, NQ - 1)]
        pltpu.make_async_copy(part, part, q_send.at[i]).wait()
    for c in range(HEAD):
        src, here, there = spot(c)
        sent, landed = src.at[pl.ds(0, NB - 1), here], buf.at[pl.ds(0, NB - 1), there]
        pltpu.make_async_copy(sent, landed, send_sem.at[c]).wait()


def shards(spectra, newest, ingest_owner, low_trial, high_trial, delay_table):
    operands = [spectra.reshape(NB, TILES, 128), newest.reshape(NB, 8, 128)]
    operands += [ingest_owner, low_trial, high_trial, delay_table]
    operands = [a if a.size == 1 else pltpu.with_memory_space_constraint(a, pltpu.HBM) for a in operands]
    state = pltpu.VMEM((NB, ROWS, 128), jnp.float32)
    table = pltpu.SMEM((LEVELS, NB), jnp.int32)
    many = pltpu.SemaphoreType.DMA((HEAD,))
    square = pltpu.VMEM((NZ, NQ, 128), jnp.float32)
    out = pl.pallas_call(
        kernel,
        out_shape=jax.ShapeDtypeStruct((NB, TILES, 128), jnp.float32),
        in_specs=[pl.BlockSpec(memory_space=pltpu.SMEM if a.size == 1 else pl.ANY) for a in operands],
        out_specs=pl.BlockSpec(memory_space=pltpu.VMEM),
        scratch_shapes=[
            state,
            pltpu.VMEM((NB, 8, 128), jnp.float32),
            pltpu.VMEM((NZ, 2 * NQ, 128), jnp.float32),
            pltpu.VMEM((NZ, 2 * NQ, 128), jnp.float32),
            square, square, square,
            pltpu.VMEM((NB, 8, 128), jnp.float32),
            pltpu.VMEM((NT, 1, 128), jnp.float32),
            pltpu.VMEM((NB, 128), jnp.float32),
            pltpu.VMEM((NB, 128), jnp.float32),
            state, state, state,
            table, table, table,
            pltpu.SemaphoreType.DMA((5,)),
            many, many,
            pltpu.SemaphoreType.DMA,
            pltpu.SemaphoreType.DMA,
            pltpu.SemaphoreType.DMA((2,)),
            pltpu.SemaphoreType.DMA((2,)),
            pltpu.SemaphoreType.DMA((NT - 1,)),
            pltpu.SemaphoreType.DMA((NT - 1,)),
            pltpu.SemaphoreType.DMA,
            pltpu.SemaphoreType.DMA,
        ],
        compiler_params=pltpu.CompilerParams(collective_id=1, has_side_effects=True, vmem_limit_bytes=24 << 20),
    )(*operands)
    return out.reshape(NB // 16, 16, TILES * 128)


def solution(mesh):
    return jax.shard_map(
        shards,
        mesh=mesh,
        in_specs=(
            P(None, "band", "tm"),
            P(None, "band", "tm", None),
            P("band"),
            P(None, "band"),
            P(None, "band"),
            P(None, "band"),
        ),
        out_specs=P("band", None, "tm"),
        check_vma=False,
    )
```

time: 148 us -> 37.4 us (0.25); the launches traced: 146 us -> 37 us
  waiting for transfers between devices: 80 us -> 0 us
  Pallas kernels: 0 us -> 35.2 us
  starting transfers between devices: 25.4 us -> 0 us
  other arithmetic: 14.5 us -> 0 us
  between operations: 14.6 us -> 0.66 us
  local copies, waits for them, and re-layouts: 11.5 us -> 1.16 us
    psum x1 -> x0, waiting for transfers between devices: 50.5 us -> none  [spread(): return lax.psum(kept, axis)]
    pallas_call x0 -> x1, Pallas kernels: none -> 35.2 us  [shards(): pl.pallas_call(kernel, out_shape=jax.ShapeDtypeStruct((NB, TILES, 128), j...]
    all_to_all x1 -> x0, waiting for transfers between devices: 28.3 us -> none  [shards(): lax.all_to_all(normed[:, None, :], 'band', split_axis=0, concat_axis=1, t...]
    ppermute x4 -> x0, starting transfers between devices: 14.9 us -> none  [from_behind(): return lax.ppermute(block, axis, route)]
    all_to_all x1 -> x0, starting transfers between devices: 10.5 us -> none  [shards(): lax.all_to_all(normed[:, None, :], 'band', split_axis=0, concat_axis=1, t...]
    gather x8 -> x0, local copies, waits for them, and re-layouts: 7.59 us -> none  [the longest x4 3.88 us: shards(): extended[odd_index]]
    select_n x21 -> x0, other arithmetic: 6.61 us -> none  [the longest x18 6.34 us: delayed_rows(): shifted = jnp.where(flags[:, None], moved, shifted)]
    mul x1 -> x0, other arithmetic: 2.4 us -> none  [shards(): normed = (spectra[:, 0, :] - block_mean[:, None]) * inv_scale[:, None]]
  transfers between devices with their start and end apart: 6 -> 0, of which waited for: 5 -> 0; matrix products, arithmetic and copies ran while one was open for 3% -> 0% of each run, Pallas kernels for 0% -> 0%
where the time goes in v3:
time: 37.4 us; the launch traced here: 37 us
  Pallas kernels  35.2 us (94%)
  local copies, waits for them, and re-layouts  1.16 us (3%)
  between operations  0.66 us (2%)
    pallas_call x1, Pallas kernels, shards(): pl.pallas_call(kernel, out_shape=jax.ShapeDtypeStruct((NB, TILES, 128), j...  35.2 us
    reshape x1, local copies, waits for them, and re-layouts, shards(): return out.reshape(NB // 16, 16, TILES * 128)  1.16 us

profile of v3, /device:TPU:64, one launch (start us, length us, event | category | flops | bytes accessed | tf_op | source)
XLA Modules:
  0.0 37.0 jit_solution(1572964594381971820)
XLA Ops:
  0.7 35.2 %shard_map.64 = f32[64,32,128]{2,1,0:T(8,128)S(1)} custom-call(f32[64,32,128]{2,1,0:T(8,128)} %bitcast.2, f32[64,8,128]{2,1,0:T(8,128)} %bitcast.3, s32[1]{0:T(128)S(6)} %copy.7.owner_ref, s32[4,64]{1,0:T(4,128)} %low_ref.1, s32[4,64]{1,0:T(4,128)} %high_ref.1, s32[4,64]{1,0:T(4,128)} %delay_ref.1), custom_call_target="tpu_custom_call" | custom-call | tf_op jit(solution)/shard_map/pallas_call | solution.py:229
  35.9 1.2 %reshape.11 = f32[4,16,4096]{2,1,0:T(8,128)} reshape(f32[64,32,128]{2,1,0:T(8,128)S(1)} %shard_map.64) | data formatting | bytes 2097152 | tf_op jit(solution)/shard_map/reshape | solution.py:259

commit v4 on v3

--- a/solution.py
+++ b/solution.py
@@ -14,9 +14,10 @@
 CHUNK = 8
 FIRST = 8
 ROWS = FIRST + TILES
-SPANS = ((0, 16), (16, 15))
-HEAD = len(SPANS)
-PLAN = [(k, c) for c in range(HEAD) for k in range(NZ)]
+BODY = TILES - 1
+GROUPS = 4
+ALL = tuple(range(NQ))
+PLAN = [(0, ALL), (1, ALL[:6]), (2, ALL[:7]), (1, ALL[6:]), (2, ALL[7:])] + [(k, ALL) for k in (3, 7, 6, 5, 4)]
 MESH = pl.DeviceIdType.MESH
 
 
@@ -48,33 +49,24 @@
     for copy in tables:
         copy.start()
 
-    def spot(c):
-        start, size = SPANS[c]
-        return x_ref, pl.ds(start, size), pl.ds(FIRST + start, size)
-
-    def send(k, c):
-        src, here, there = spot(c)
-
+    def send(k, turns):
         def one(peer):
             pltpu.make_async_remote_copy(
-                src_ref=src.at[peer, here], dst_ref=buf.at[me, there], send_sem=send_sem.at[c],
-                recv_sem=recv_sem.at[c], device_id={"band": peer}, device_id_type=MESH,
+                src_ref=x_ref.at[peer, pl.ds(0, BODY)], dst_ref=buf.at[me, pl.ds(FIRST, BODY)], send_sem=send_sem,
+                recv_sem=recv_sem.at[z // 2], device_id={"band": peer}, device_id_type=MESH,
             ).start()
 
-        pl.when(k != z)(lambda: one(k * NQ + q))
-        for r in range(1, NQ):
-            one(k * NQ + turned[r])
-
-    def keep_own(c):
-        src, here, there = spot(c)
-        pltpu.make_async_copy(src.at[me, here], buf.at[me, there], recv_sem.at[c]).start()
-
-    def arrive(c):
-        src, here, there = spot(c)
-        pltpu.make_async_copy(src.at[:, here], buf.at[:, there], recv_sem.at[c]).wait()
-
-    for c in range(HEAD):
-        keep_own(c)
+        for r in turns:
+            if r == 0:
+                pl.when(k != z)(lambda: one(k * NQ + q))
+            else:
+                one(k * NQ + turned[r])
+
+    def arrive(g):
+        rows = buf.at[pl.ds(g * 16, 16), pl.ds(FIRST, BODY)]
+        pltpu.make_async_copy(rows, rows, recv_sem.at[g]).wait()
+
+    pltpu.make_async_copy(x_ref.at[me, pl.ds(0, BODY)], buf.at[me, pl.ds(FIRST, BODY)], recv_sem.at[z // 2]).start()
 
     row = lax.broadcasted_iota(jnp.int32, (NB, 128), 0)
     column = lax.broadcasted_iota(jnp.int32, (NB, 128), 1)
@@ -109,8 +101,8 @@
             recv_sem=z_recv, device_id={"band": k * NQ + q}, device_id_type=MESH,
         ))
         head_copies[-1].start()
-    for k, c in PLAN:
-        send(k, c)
+    for k, turns in PLAN:
+        send(k, turns)
     head[z, pl.ds(0, NQ + 1)] = packed[z, pl.ds(0, NQ + 1)]
 
     lane = lax.broadcasted_iota(jnp.int32, (CHUNK, 128), 1)
@@ -127,10 +119,12 @@
         base = r // (2 * half) * (2 * half)
         return base + low[level, r], base + half + high[level, r]
 
-    def levels(blocks):
-        nows = [pl.ds(FIRST + block * CHUNK, CHUNK) for block in blocks]
-        befores = [pl.ds(FIRST + block * CHUNK - 1, CHUNK) for block in blocks]
-        for even in range(0, NB, 2):
+    blocks = range(TILES // CHUNK)
+    nows = [pl.ds(FIRST + block * CHUNK, CHUNK) for block in blocks]
+    befores = [pl.ds(FIRST + block * CHUNK - 1, CHUNK) for block in blocks]
+
+    def levels(g):
+        for even in range(g * 16, g * 16 + 16, 2):
             for block, now, before in zip(blocks, nows, befores):
                 base, n_now, n_before = normed(even, now), normed(even + 1, now), normed(even + 1, before)
                 if block == 0:
@@ -138,7 +132,7 @@
                 for k in range(2):
                     s1[even + k, now] = base + delayed(n_now, n_before, delay[0, even + k])
         for level, src, dst in ((1, s1, s2), (2, s2, s3), (3, s3, None)):
-            for r in range(NB):
+            for r in range(g * 16, g * 16 + 16):
                 lo, hi = pick(level, r)
                 for block, now, before in zip(blocks, nows, befores):
                     value = src[lo, now] + delayed(src[hi, now], src[hi, before], delay[level, r])
@@ -201,9 +195,14 @@
     buf[:, FIRST - 1, :] = before_first[...].reshape(NB, 128)
     buf[:, ROWS - 1, :] = tiles[...].reshape(NB, 128)
     halo_levels()
-    for c, (start, size) in enumerate(SPANS):
-        arrive(c)
-        levels(range(start // CHUNK, (start + size + 1) // CHUNK))
+    def merge(order):
+        for g in order:
+            arrive(g)
+            levels(g)
+
+    far_last = (z < NZ // 2) | (z == 5)
+    pl.when(far_last)(lambda: merge((0, 1, 2, 3)))
+    pl.when(jnp.logical_not(far_last))(lambda: merge((3, 2, 0, 1)))
 
     halo.wait_send()
     for copy in t_copies:
@@ -212,10 +211,8 @@
     for i, dst in enumerate((tiles, stat_q)):
         part = dst.at[:, pl.ds(0, NQ - 1)]
         pltpu.make_async_copy(part, part, q_send.at[i]).wait()
-    for c in range(HEAD):
-        src, here, there = spot(c)
-        sent, landed = src.at[pl.ds(0, NB - 1), here], buf.at[pl.ds(0, NB - 1), there]
-        pltpu.make_async_copy(sent, landed, send_sem.at[c]).wait()
+    rows = buf.at[pl.ds(0, NB - 1), pl.ds(FIRST, BODY)]
+    pltpu.make_async_copy(rows, rows, send_sem).wait()
 
 
 def shards(spectra, newest, ingest_owner, low_trial, high_trial, delay_table):
@@ -224,7 +221,6 @@
     operands = [a if a.size == 1 else pltpu.with_memory_space_constraint(a, pltpu.HBM) for a in operands]
     state = pltpu.VMEM((NB, ROWS, 128), jnp.float32)
     table = pltpu.SMEM((LEVELS, NB), jnp.int32)
-    many = pltpu.SemaphoreType.DMA((HEAD,))
     square = pltpu.VMEM((NZ, NQ, 128), jnp.float32)
     out = pl.pallas_call(
         kernel,
@@ -244,7 +240,8 @@
             state, state, state,
             table, table, table,
             pltpu.SemaphoreType.DMA((5,)),
-            many, many,
+            pltpu.SemaphoreType.DMA,
+            pltpu.SemaphoreType.DMA((GROUPS,)),
             pltpu.SemaphoreType.DMA,
             pltpu.SemaphoreType.DMA,
             pltpu.SemaphoreType.DMA((2,)),

time: 37.4 us -> 36.2 us (0.968)
  Pallas kernels: 35.2 us -> 34 us
    pallas_call x1, Pallas kernels: 35.2 us -> 34 us  [shards(): pl.pallas_call(kernel, out_shape=jax.ShapeDtypeStruct((NB, TILES, 128), j...]
where the time goes in v4:
time: 36.2 us; the launch traced here: 35.8 us
  Pallas kernels  34 us (94%)
  local copies, waits for them, and re-layouts  1.16 us (3%)
  between operations  0.66 us (2%)
    pallas_call x1, Pallas kernels, shards(): pl.pallas_call(kernel, out_shape=jax.ShapeDtypeStruct((NB, TILES, 128), j...  34 us
    reshape x1, local copies, waits for them, and re-layouts, shards(): return out.reshape(NB // 16, 16, TILES * 128)  1.16 us

profile of v4, /device:TPU:64, one launch (start us, length us, event | category | flops | bytes accessed | tf_op | source)
XLA Modules:
  0.0 35.8 jit_solution(7079428084743259568)
XLA Ops:
  0.7 34.0 %shard_map.64 = f32[64,32,128]{2,1,0:T(8,128)S(1)} custom-call(f32[64,32,128]{2,1,0:T(8,128)} %bitcast.2, f32[64,8,128]{2,1,0:T(8,128)} %bitcast.3, s32[1]{0:T(128)S(6)} %copy.7.owner_ref, s32[4,64]{1,0:T(4,128)} %low_ref.1, s32[4,64]{1,0:T(4,128)} %high_ref.1, s32[4,64]{1,0:T(4,128)} %delay_ref.1), custom_call_target="tpu_custom_call" | custom-call | tf_op jit(solution)/shard_map/pallas_call | solution.py:225
  34.7 1.2 %reshape.11 = f32[4,16,4096]{2,1,0:T(8,128)} reshape(f32[64,32,128]{2,1,0:T(8,128)S(1)} %shard_map.64) | data formatting | bytes 2097152 | tf_op jit(solution)/shard_map/reshape | solution.py:256

commit v5 on v4

--- a/solution.py
+++ b/solution.py
@@ -32,7 +32,7 @@
     barrier = pltpu.get_barrier_semaphore()
     turned = [jnp.where(q + r < NQ, q + r, q + r - NQ) for r in range(NQ)]
     t_peers = [jnp.where(t + i < NT, t + i, t + i - NT) for i in range(1, NT)]
-    for i in range(1, NB):
+    for i in sorted(range(1, NB), key=lambda i: abs(i - NB // 2)):
         peer = jnp.where(me + i < NB, me + i, me + i - NB)
         pl.semaphore_signal(barrier, inc=1, device_id={"band": peer}, device_id_type=MESH)
     for k in t_peers:
@@ -195,8 +195,19 @@
     buf[:, FIRST - 1, :] = before_first[...].reshape(NB, 128)
     buf[:, ROWS - 1, :] = tiles[...].reshape(NB, 128)
     halo_levels()
+    def settle():
+        halo.wait_send()
+        for copy in t_copies:
+            copy.wait_send()
+        pltpu.make_async_copy(landed, landed, z_send).wait()
+        for i, dst in enumerate((tiles, stat_q)):
+            part = dst.at[:, pl.ds(0, NQ - 1)]
+            pltpu.make_async_copy(part, part, q_send.at[i]).wait()
+
     def merge(order):
         for g in order:
+            if g == order[-1]:
+                settle()
             arrive(g)
             levels(g)
 
@@ -204,13 +215,6 @@
     pl.when(far_last)(lambda: merge((0, 1, 2, 3)))
     pl.when(jnp.logical_not(far_last))(lambda: merge((3, 2, 0, 1)))
 
-    halo.wait_send()
-    for copy in t_copies:
-        copy.wait_send()
-    pltpu.make_async_copy(landed, landed, z_send).wait()
-    for i, dst in enumerate((tiles, stat_q)):
-        part = dst.at[:, pl.ds(0, NQ - 1)]
-        pltpu.make_async_copy(part, part, q_send.at[i]).wait()
     rows = buf.at[pl.ds(0, NB - 1), pl.ds(FIRST, BODY)]
     pltpu.make_async_copy(rows, rows, send_sem).wait()
 

time: 36.2 us -> 36.2 us (level)
  no operation moved by 1% of the time
where the time goes in v5:
time: 36.2 us; the launch traced here: 35.8 us
  Pallas kernels  34 us (94%)
  local copies, waits for them, and re-layouts  1.16 us (3%)
  between operations  0.66 us (2%)
    pallas_call x1, Pallas kernels, shards(): pl.pallas_call(kernel, out_shape=jax.ShapeDtypeStruct((NB, TILES, 128), j...  34 us
    reshape x1, local copies, waits for them, and re-layouts, shards(): return out.reshape(NB // 16, 16, TILES * 128)  1.16 us

profile of v5, /device:TPU:64, one launch (start us, length us, event | category | flops | bytes accessed | tf_op | source)
XLA Modules:
  0.0 35.8 jit_solution(10366773781718669422)
XLA Ops:
  0.7 34.0 %shard_map.64 = f32[64,32,128]{2,1,0:T(8,128)S(1)} custom-call(f32[64,32,128]{2,1,0:T(8,128)} %bitcast.2, f32[64,8,128]{2,1,0:T(8,128)} %bitcast.3, s32[1]{0:T(128)S(6)} %copy.7.owner_ref, s32[4,64]{1,0:T(4,128)} %low_ref.1, s32[4,64]{1,0:T(4,128)} %high_ref.1, s32[4,64]{1,0:T(4,128)} %delay_ref.1), custom_call_target="tpu_custom_call" | custom-call | tf_op jit(solution)/shard_map/pallas_call | solution.py:229
  34.6 1.2 %reshape.11 = f32[4,16,4096]{2,1,0:T(8,128)} reshape(f32[64,32,128]{2,1,0:T(8,128)S(1)} %shard_map.64) | data formatting | bytes 2097152 | tf_op jit(solution)/shard_map/reshape | solution.py:260

commit v6 on v5

--- a/solution.py
+++ b/solution.py
@@ -16,8 +16,8 @@
 ROWS = FIRST + TILES
 BODY = TILES - 1
 GROUPS = 4
-ALL = tuple(range(NQ))
-PLAN = [(0, ALL), (1, ALL[:6]), (2, ALL[:7]), (1, ALL[6:]), (2, ALL[7:])] + [(k, ALL) for k in (3, 7, 6, 5, 4)]
+ALL = (4, 5, 2, 3, 6, 7, 0, 1)
+PLAN = [(0, ALL), (1, ALL), (2, ALL)] + [(k, ALL) for k in (3, 7, 6, 5, 4)]
 MESH = pl.DeviceIdType.MESH
 
 

time: 36.2 us -> 36.3 us (level)
  Pallas kernels: 34 us -> 34.4 us
    pallas_call x1, Pallas kernels: 34 us -> 34.4 us  [shards(): pl.pallas_call(kernel, out_shape=jax.ShapeDtypeStruct((NB, TILES, 128), j...]
where the time goes in v6:
time: 36.3 us; the launch traced here: 36.2 us
  Pallas kernels  34.4 us (95%)
  local copies, waits for them, and re-layouts  1.16 us (3%)
  between operations  0.66 us (2%)
    pallas_call x1, Pallas kernels, shards(): pl.pallas_call(kernel, out_shape=jax.ShapeDtypeStruct((NB, TILES, 128), j...  34.4 us
    reshape x1, local copies, waits for them, and re-layouts, shards(): return out.reshape(NB // 16, 16, TILES * 128)  1.16 us

profile of v6, /device:TPU:64, one launch (start us, length us, event | category | flops | bytes accessed | tf_op | source)
XLA Modules:
  0.0 36.2 jit_solution(4665236707498259293)
XLA Ops:
  0.7 34.4 %shard_map.64 = f32[64,32,128]{2,1,0:T(8,128)S(1)} custom-call(f32[64,32,128]{2,1,0:T(8,128)} %bitcast.2, f32[64,8,128]{2,1,0:T(8,128)} %bitcast.3, s32[1]{0:T(128)S(6)} %copy.7.owner_ref, s32[4,64]{1,0:T(4,128)} %low_ref.1, s32[4,64]{1,0:T(4,128)} %high_ref.1, s32[4,64]{1,0:T(4,128)} %delay_ref.1), custom_call_target="tpu_custom_call" | custom-call | tf_op jit(solution)/shard_map/pallas_call | solution.py:229
  35.1 1.2 %reshape.11 = f32[4,16,4096]{2,1,0:T(8,128)} reshape(f32[64,32,128]{2,1,0:T(8,128)S(1)} %shard_map.64) | data formatting | bytes 2097152 | tf_op jit(solution)/shard_map/reshape | solution.py:260
